TPU v7x, 32 devices: a whole 2x2x4 slice. The times are simulated.
32 devices in a mesh: dp: 16 (over z, y, core), tensor: 2 (over x).
Axes of the slice: x: 2, y: 2, z: 4, core: 2. Of those that a mesh axis runs over, the one named last changes fastest.
Arguments:
- tokens: bfloat16 [6144, 4096], P(('dp', 'tensor')), may hold values from -21 to 21
- wq_codes: bfloat16 [4096, 1024], P('dp', 'tensor'), may hold values from -4 to 4
- wq_scales: float32 [32, 8], replicated, may hold values from 0.0078125 to 0.03125
- wk_codes: bfloat16 [4096, 128], P('dp', 'tensor'), may hold values from -4 to 4
- wk_scales: float32 [32, 1], replicated, may hold values from 0.0078125 to 0.03125
- wv_codes: bfloat16 [4096, 128], P('dp', 'tensor'), may hold values from -4 to 4
- wv_scales: float32 [32, 1], replicated, may hold values from 0.0078125 to 0.03125
- wo_codes: bfloat16 [1024, 4096], P('tensor', 'dp'), may hold values from -4 to 4
- wo_scales: float32 [8, 32], replicated, may hold values from 0.015625 to 0.0625
Outputs:
- mixed: bfloat16 [6144, 4096], P(('dp', 'tensor'))
All inputs are finite; a program needn't handle non-finite values.
Results may differ from a plain program's by a relative error of at most 0.014.
The roundings to bfloat16 on the way count: a program that leaves them out, or rounds other values in their place, can miss the bound.
Values may be sent and summed in bfloat16 or wider, within the bound.
A program may use at most 64 MiB of HBM per device.

v0:
```python
import jax
import jax.numpy as jnp
from jax import lax
from jax.sharding import PartitionSpec as P

HEAD = 128
BLOCK = 128
SPAN = 384
rope_base = 500000.0
masked_value = -1e30


def from_partner(value, axis, apart):
    mask = 2**apart
    pairs = [(source, source ^ mask) for source in range(lax.axis_size(axis))]
    return lax.ppermute(value, axis, pairs)


def dequantize(codes, scales, row_start, col_start):
    height, breadth = codes.shape
    row_block = (row_start + jnp.arange(height, dtype=jnp.int32)) // BLOCK
    col_block = (col_start + jnp.arange(breadth, dtype=jnp.int32)) // BLOCK
    row_pick = (row_block[:, None] == jnp.arange(scales.shape[0], dtype=jnp.int32)[None, :]).astype(
        jnp.float32
    )
    col_pick = (col_block[None, :] == jnp.arange(scales.shape[1], dtype=jnp.int32)[:, None]).astype(
        jnp.float32
    )
    picked = jnp.dot(row_pick, scales, precision=lax.Precision.HIGHEST)
    expanded = jnp.dot(picked, col_pick, precision=lax.Precision.HIGHEST)
    return (codes.astype(jnp.float32) * expanded).astype(jnp.bfloat16)


def rotate(features, positions):
    half_size = HEAD // 2
    steps = jnp.arange(half_size).astype(jnp.float32)
    inverse = jnp.exp(-(2.0 * steps / HEAD) * jnp.log(jnp.float32(rope_base)))
    angle = positions[:, None] * inverse[None, :]
    cosine = jnp.cos(angle)[:, None, :]
    sine = jnp.sin(angle)[:, None, :]
    first = features[..., :half_size]
    second = features[..., half_size:]
    return jnp.concatenate(
        [first * cosine - second * sine, second * cosine + first * sine], axis=-1
    )


def in_order(upper, mine, partner):
    return jnp.where(
        upper, jnp.concatenate([partner, mine], axis=1), jnp.concatenate([mine, partner], axis=1)
    )


def body(
    tokens, wq_codes, wq_scales, wk_codes, wk_scales, wv_codes, wv_scales, wo_codes, wo_scales
):
    data_index = lax.axis_index("dp")
    head_index = lax.axis_index("tensor")
    weight_rows = wq_codes.shape[0]
    row_start = data_index * weight_rows
    query_width = wq_codes.shape[1]
    shard_width = wk_codes.shape[1]
    wq_local = dequantize(wq_codes, wq_scales, row_start, head_index * query_width)
    wk_local = dequantize(wk_codes, wk_scales, row_start, head_index * shard_width)
    wv_local = dequantize(wv_codes, wv_scales, row_start, head_index * shard_width)
    wo_local = dequantize(
        wo_codes, wo_scales, head_index * wo_codes.shape[0], data_index * wo_codes.shape[1]
    )
    wo_whole = lax.all_gather(wo_local, "dp", axis=1, tiled=True)
    sequence = lax.all_gather(tokens, "tensor", axis=0, tiled=True)
    upper = head_index % 2 == 1
    partner_k, partner_v = from_partner((wk_local, wv_local), "tensor", 0)
    wk_used = in_order(upper, wk_local, partner_k)
    wv_used = in_order(upper, wv_local, partner_v)
    length = sequence.shape[0]
    full_q, full_k, full_v = (
        lax.all_gather(wq_local, "dp", axis=0, tiled=True),
        lax.all_gather(wk_used, "dp", axis=0, tiled=True),
        lax.all_gather(wv_used, "dp", axis=0, tiled=True),
    )
    query_lin = jnp.dot(sequence, full_q, preferred_element_type=jnp.float32)
    key_lin = jnp.dot(sequence, full_k, preferred_element_type=jnp.float32)
    value_lin = jnp.dot(sequence, full_v, preferred_element_type=jnp.float32)
    positions = (jnp.arange(length) % SPAN).astype(jnp.float32)
    heads_here = query_width // HEAD
    span_count = length // SPAN
    queries = rotate(query_lin.reshape(length, heads_here, HEAD), positions).astype(jnp.bfloat16)
    keys = rotate(key_lin.reshape(length, 1, HEAD), positions)[:, 0, :].astype(jnp.bfloat16)
    values = value_lin.astype(jnp.bfloat16)
    queries = queries.reshape(span_count, SPAN, heads_here, HEAD)
    keys = keys.reshape(span_count, SPAN, HEAD)
    values = values.reshape(span_count, SPAN, HEAD)
    causal = jnp.arange(SPAN)[:, None] >= jnp.arange(SPAN)[None, :]
    scores = jnp.einsum("cqhd,ckd->chqk", queries, keys, preferred_element_type=jnp.float32) * (
        1.0 / HEAD**0.5
    )
    scores = jnp.where(causal[None, None, :, :], scores, masked_value)
    peak = jnp.max(scores, axis=-1, keepdims=True)
    powers = jnp.exp(scores - peak)
    total = jnp.sum(powers, axis=-1, keepdims=True)
    probs = (powers / total).astype(jnp.bfloat16)
    attended = (
        jnp.einsum("chqk,ckd->cqhd", probs, values, preferred_element_type=jnp.float32)
        .astype(jnp.bfloat16)
        .reshape(length, query_width)
    )
    terms = jnp.dot(attended, wo_whole, preferred_element_type=jnp.float32)
    mixed = lax.psum_scatter(terms.astype(jnp.bfloat16), "tensor", scatter_dimension=0, tiled=True)
    return mixed


def solution(mesh):
    return jax.shard_map(
        body,
        mesh=mesh,
        in_specs=(
            P(("dp", "tensor"), None),
            P("dp", "tensor"),
            P(),
            P("dp", "tensor"),
            P(),
            P("dp", "tensor"),
            P(),
            P("tensor", "dp"),
            P(),
        ),
        out_specs=P(("dp", "tensor"), None),
        check_vma=False,
    )
```

profile of v0, /device:TPU:0, one launch (start us, length us, event | category | flops | bytes accessed | tf_op | source)
XLA Modules:
  0.0 298.7 jit_solution(14492165854905876810)
XLA Ops:
  6.6 0.9 fusion.18
  7.5 0.9 fusion.17
  8.4 0.9 multiply_convert_fusion.1
  9.3 3.0 %collective-permute-start.1 = (bf16[256,64]{0,1:T(8,128)(2,1)S(1)}, bf16[256,64]{0,1:T(8,128)(2,1)S(1)}, u32[]{:S(2)}, u32[]{:S(2)}) collective-permute-start(bf16[256,64]{0,1:T(8,128)(2,1)S(1)} %get-tuple-element.14), channel_id=1, source_target_pairs={{0,1},{1,0},{2,3},{3,2},{4,5},{5,4},{6,7},{7,6},{8,9},{9,8},{10,11... | collective-permute-start | bytes 98312 | tf_op jit(solution)/shard_map/ppermute | solution.py:16
  12.3 1.9 collective-permute-done.1
  14.2 0.6 maximum_select_fusion.1
  14.9 0.7 all-gather.8.cloned.1.call-update
  15.7 0.9 fusion.16
  16.7 1.1 fusion.2
  17.8 2.1 collective-permute-start
  19.9 1.9 collective-permute-done
  21.8 0.6 maximum_select_fusion
  22.5 0.3 fusion.10
  22.8 1.1 fusion.3
  24.1 1.4 multiply_cosine_fusion
  25.5 28.1 %all-gather.10.cloned.1.call-done = bf16[4096,128]{0,1:T(8,128)(2,1)} async-done(((bf16[256,128]{0,1:T(8,128)(2,1)}), bf16[4096,128]{0,1:T(8,128)(2,1)}) %all-gather.10.cloned.1.call-update) | async-done | bytes 1048592 | tf_op jit(solution)/shard_map/all_gather | solution.py:78
  53.6 46.0 %all-gather.8.cloned.1.call-done = bf16[384,4096]{1,0:T(8,128)(2,1)} async-done(((bf16[192,4096]{1,0:T(8,128)(2,1)}), bf16[384,4096]{1,0:T(8,128)(2,1)}) %all-gather.8.cloned.1.call-update) | async-done | bytes 3145744 | tf_op jit(solution)/shard_map/all_gather | solution.py:70
  99.6 3.4 %convolution_bitcast_fusion = f32[384,1,128]{0,2,1:T(8,128)S(1)} fusion(bf16[4096,128]{0,1:T(8,128)(2,1)} %all-gather.10.cloned.1.call-done, bf16[384,4096]{1,0:T(8,128)(2,1)} %all-gather.8.cloned.1.call-done), kind=kOutput, calls=%fused_computation.12 | convolution fusion | flops 402653184 | bytes 4390912 | tf_op jit(solution)/shard_map/dot_general | solution.py:82
  103.1 1.1 fusion.20
  104.1 48.3 %all-gather.12.cloned.1.call-done = bf16[4096,512]{1,0:T(8,128)(2,1)} async-done(((bf16[256,512]{1,0:T(8,128)(2,1)}), bf16[4096,512]{1,0:T(8,128)(2,1)}) %all-gather.12.cloned.1.call-update) | async-done | bytes 4194320 | tf_op jit(solution)/shard_map/all_gather | solution.py:77
  152.4 4.6 %fusion.37 = f32[512,384]{1,0:T(8,128)S(1)} fusion(bf16[4096,512]{1,0:T(8,128)(2,1)} %all-gather.12.cloned.1.call-done, bf16[384,4096]{1,0:T(8,128)(2,1)S(1)} %copy-done.1), kind=kOutput, calls=%fused_computation.79 | convolution fusion | flops 1610612736 | bytes 8126464 | tf_op jit(solution)/shard_map/dot_general | solution.py:81
  157.1 0.3 copy.17
  157.4 0.3 copy.18
  157.6 0.3 copy-done.2
  157.9 0.2 subtract_convert_fusion
  158.2 0.7 fusion.1
  158.9 0.5 fusion
  159.4 30.4 %all-gather.6.cloned.1.call-done = bf16[4096,128]{0,1:T(8,128)(2,1)} async-done(((bf16[256,128]{0,1:T(8,128)(2,1)}), bf16[4096,128]{0,1:T(8,128)(2,1)}) %all-gather.6.cloned.1.call-update) | async-done | bytes 1048592 | tf_op jit(solution)/shard_map/all_gather | solution.py:79
  189.7 4.1 %convolution_convert_fusion.1 = bf16[128,4,384]{2,0,1:T(8,128)(2,1)S(1)} fusion(f32[384,384,4]{1,0,2:T(8,128)S(1)} %get-tuple-element.16, f32[4,384]{1,0:T(4,128)S(1)} %fusion, f32[4,384]{1,0:T(4,128)S(1)} %get-tuple-element.15, pred[384,384]{0,1:T(8,128)(4,1)S(1)} %iota_compare_fusion, bf16[4096,128]{0,1:T(8,128)(2,1)} %all-gather.6.cloned.1.call-done, ...), kind=kOutput, calls=%fused_computation.6 | convolution fusion | flops 556843008 | bytes 7106560 | tf_op jit(solution)/shard_map/chqk,ckd->cqhd/dot_general | solution.py:103
  193.8 50.7 %all-gather.14.cloned.1.call-done = bf16[512,4096]{1,0:T(8,128)(2,1)} async-done(((bf16[512,256]{1,0:T(8,128)(2,1)}), bf16[512,4096]{1,0:T(8,128)(2,1)}) %all-gather.14.cloned.1.call-update) | async-done | bytes 4194320 | tf_op jit(solution)/shard_map/all_gather | solution.py:69
  244.5 5.7 %convolution_convert_fusion = bf16[384,4096]{1,0:T(8,128)(2,1)} fusion(bf16[384,512]{0,1:T(8,128)(2,1)S(1)} %bitcast.58, bf16[512,4096]{1,0:T(8,128)(2,1)} %all-gather.14.cloned.1.call-done), kind=kOutput, calls=%fused_computation | convolution fusion | flops 1612185600 | bytes 7733248 | tf_op jit(solution)/shard_map/dot_general | solution.py:107
  250.2 41.7 %reduce-scatter.2.cloned.1.call-done = bf16[192,4096]{1,0:T(8,128)(2,1)} async-done(((bf16[384,4096]{1,0:T(8,128)(2,1)}), bf16[192,4096]{1,0:T(8,128)(2,1)}) %reduce-scatter.2.cloned.1.call-update) | async-done | bytes 1572880 | tf_op jit(solution)/shard_map/reduce_scatter | solution.py:108
  (29 shorter events, 0.5 us)
Async XLA Ops:
  6.5 16.0 %copy-start = (f32[8,32]{1,0:T(8,128)S(1)}, f32[8,32]{1,0:T(8,128)}, u32[]{:S(2)}) copy-start(f32[8,32]{1,0:T(8,128)} %param.17) | copy-start | bytes 3076
  6.5 10.1 %copy-start.3 = (bf16[256,512]{1,0:T(8,128)(2,1)S(1)}, bf16[256,512]{1,0:T(8,128)(2,1)}, u32[]{:S(2)}) copy-start(bf16[256,512]{1,0:T(8,128)(2,1)} %param.10) | copy-start | bytes 786436
  6.5 16.3 %copy-start.4 = (bf16[512,256]{1,0:T(8,128)(2,1)S(1)}, bf16[512,256]{1,0:T(8,128)(2,1)}, u32[]{:S(2)}) copy-start(bf16[512,256]{1,0:T(8,128)(2,1)} %param.16) | copy-start | bytes 786436
  6.5 47.1 %all-gather.10.cloned.1.call-start = ((), (), s32[]{:S(2)}) async-start(), calls=%async_computation.3 | async-start | bytes 1114112 | tf_op jit(solution)/shard_map/all_gather | solution.py:78
  9.3 4.9 %collective-permute-start.1 = (bf16[256,64]{0,1:T(8,128)(2,1)S(1)}, bf16[256,64]{0,1:T(8,128)(2,1)S(1)}, u32[]{:S(2)}, u32[]{:S(2)}) collective-permute-start(bf16[256,64]{0,1:T(8,128)(2,1)S(1)} %get-tuple-element.14), channel_id=1, source_target_pairs={{0,1},{1,0},{2,3},{3,2},{4,5},{5,4},{6,7},{7,6},{8,9},{9,8},{10,11... | collective-permute-start | bytes 98312 | tf_op jit(solution)/shard_map/ppermute | solution.py:16
  14.9 84.7 %all-gather.8.cloned.1.call-start = ((), (), s32[]{:S(2)}) async-start(), calls=%async_computation.2 | async-start | bytes 4718592 | tf_op jit(solution)/shard_map/all_gather | solution.py:70
  15.6 136.8 %all-gather.12.cloned.1.call-start = ((), (), s32[]{:S(2)}) async-start(), calls=%async_computation.4 | async-start | bytes 4456448 | tf_op jit(solution)/shard_map/all_gather | solution.py:77
  17.8 172.0 %all-gather.6.cloned.1.call-start = ((), (), s32[]{:S(2)}) async-start(), calls=%async_computation.1 | async-start | bytes 1114112 | tf_op jit(solution)/shard_map/all_gather | solution.py:79
  17.8 4.0 %collective-permute-start = (bf16[256,64]{0,1:T(8,128)(2,1)S(1)}, bf16[256,64]{0,1:T(8,128)(2,1)S(1)}, u32[]{:S(2)}, u32[]{:S(2)}) collective-permute-start(bf16[256,64]{0,1:T(8,128)(2,1)S(1)} %get-tuple-element.13), channel_id=1, source_target_pairs={{0,1},{1,0},{2,3},{3,2},{4,5},{5,4},{6,7},{7,6},{8,9},{9,8},{10,11... | collective-permute-start | bytes 98312 | tf_op jit(solution)/shard_map/ppermute | solution.py:16
  22.4 222.0 %all-gather.14.cloned.1.call-start = ((), (), s32[]{:S(2)}) async-start(), calls=%async_computation.5 | async-start | bytes 4456448 | tf_op jit(solution)/shard_map/all_gather | solution.py:69
  23.9 267.9 %reduce-scatter.2.cloned.1.call-start = ((), (), s32[]{:S(2)}) async-start(), calls=%async_computation.6 | async-start | bytes 4718592 | tf_op jit(solution)/shard_map/reduce_scatter | solution.py:108
  99.6 52.8 %copy-start.1 = (bf16[384,4096]{1,0:T(8,128)(2,1)S(1)}, bf16[384,4096]{1,0:T(8,128)(2,1)}, u32[]{:S(2)}) copy-start(bf16[384,4096]{1,0:T(8,128)(2,1)} %all-gather.8.cloned.1.call-done) | copy-start | bytes 9437188
  157.0 0.9 copy-start.2
  157.1 1.1 copy-start.5
Sparse Core Ops, SparseCore 0:
  15.0 38.5 all-gather.9
  55.2 44.4 all-gather.7
  101.8 50.5 all-gather.11
  154.4 35.2 all-gather.5
  191.7 52.6 all-gather.13
  250.3 41.4 reduce-scatter.1
where the time goes:
time: 299 us
  waiting for transfers between devices  250 us (84%)
  matrix products  23.7 us (8%)
  between operations  13.7 us (5%)
  other arithmetic  5.51 us (2%)
  starting transfers between devices  5.3 us (2%)
    all_gather x1, waiting for transfers between devices, body(): wo_whole = lax.all_gather(wo_local, 'dp', axis=1, tiled=True)  50.7 us
    all_gather x1, waiting for transfers between devices, body(): lax.all_gather(wq_local, 'dp', axis=0, tiled=True)  48.3 us
    all_gather x1, waiting for transfers between devices, body(): sequence = lax.all_gather(tokens, 'tensor', axis=0, tiled=True)  46 us
    reduce_scatter x1, waiting for transfers between devices, body(): lax.psum_scatter(terms.astype(jnp.bfloat16), 'tensor', scatter_dimension=...  41.7 us
    all_gather x1, waiting for transfers between devices, body(): lax.all_gather(wv_used, 'dp', axis=0, tiled=True)  30.4 us
    all_gather x1, waiting for transfers between devices, body(): lax.all_gather(wk_used, 'dp', axis=0, tiled=True)  28.1 us
  transfers between devices with their start and end apart: 8, of which 8 were waited for; matrix products, arithmetic and copies ran while one was open for 7% of the time, Pallas kernels for 0%

commit v1 on v0

--- a/solution.py
+++ b/solution.py
@@ -66,7 +66,13 @@
     wo_local = dequantize(
         wo_codes, wo_scales, head_index * wo_codes.shape[0], data_index * wo_codes.shape[1]
     )
-    wo_whole = lax.all_gather(wo_local, "dp", axis=1, tiled=True)
+    size = lax.axis_size("dp")
+    held, blocks = (wo_local, [wo_local])
+    for _ in range(size - 1):
+        held = lax.ppermute(held, "dp", [(i, (i + 1) % size) for i in range(size)])
+        blocks.insert(0, held)
+    line = jnp.concatenate(blocks, axis=1)
+    wo_whole = jnp.roll(line, (lax.axis_index("dp") + 1) * wo_local.shape[1], axis=1)
     sequence = lax.all_gather(tokens, "tensor", axis=0, tiled=True)
     upper = head_index % 2 == 1
     partner_k, partner_v = from_partner((wk_local, wv_local), "tensor", 0)

time: 299 us -> 269 us (0.90)
  waiting for transfers between devices: 250 us -> 176 us
  local copies, waits for them, and re-layouts: 0.91 us -> 42.8 us
    ppermute x0 -> x15, waiting for transfers between devices: none -> 133 us  [body(): held = lax.ppermute(held, 'dp', [(i, (i + 1) % size) for i in range(size)])]
    all_gather x1 -> x0, waiting for transfers between devices: 50.7 us -> none  [body(): wo_whole = lax.all_gather(wo_local, 'dp', axis=1, tiled=True)]
    all_gather x1, waiting for transfers between devices: 48.3 us -> 0.01 us  [body(): lax.all_gather(wq_local, 'dp', axis=0, tiled=True)]
    all_gather x1, waiting for transfers between devices: 46 us -> 0.01 us  [body(): sequence = lax.all_gather(tokens, 'tensor', axis=0, tiled=True)]
    unnamed x14 -> x90, local copies, waits for them, and re-layouts: 0.85 us -> 42 us
    all_gather x1, waiting for transfers between devices: 30.4 us -> 0.02 us  [body(): lax.all_gather(wv_used, 'dp', axis=0, tiled=True)]
    all_gather x1, waiting for transfers between devices: 28.1 us -> 0.01 us  [body(): lax.all_gather(wk_used, 'dp', axis=0, tiled=True)]
  transfers between devices with their start and end apart: 8 -> 22, of which waited for: 8 -> 17; matrix products, arithmetic and copies ran while one was open for 7% -> 19% of each run, Pallas kernels for 0% -> 0%
where the time goes in v1:
time: 269 us
  waiting for transfers between devices  176 us (65%)
  local copies, waits for them, and re-layouts  42.8 us (16%)
  matrix products  24.1 us (9%)
  between operations  13.4 us (5%)
  other arithmetic  6.7 us (2%)
  starting transfers between devices  5.64 us (2%)
    ppermute x15, waiting for transfers between devices, body(): held = lax.ppermute(held, 'dp', [(i, (i + 1) % size) for i in range(size)])  133 us
    unnamed x90, local copies, waits for them, and re-layouts  42 us
    reduce_scatter x1, waiting for transfers between devices, body(): lax.psum_scatter(terms.astype(jnp.bfloat16), 'tensor', scatter_dimension=...  40.7 us
    dot_general x1, matrix products, body(): terms = jnp.dot(attended, wo_whole, preferred_element_type=jnp.float32)  5.74 us
    ppermute x2, starting transfers between devices, from_partner(): return lax.ppermute(value, axis, pairs)  5.38 us
  transfers between devices with their start and end apart: 22, of which 17 were waited for; matrix products, arithmetic and copies ran while one was open for 19% of the time, Pallas kernels for 0%

profile of v1, /device:TPU:0, one launch (start us, length us, event | category | flops | bytes accessed | tf_op | source)
XLA Modules:
  0.0 268.7 jit_solution(7116009893303308626)
XLA Ops:
  9.3 3.0 %collective-permute-start.1 = (bf16[256,64]{0,1:T(8,128)(2,1)S(1)}, bf16[256,64]{0,1:T(8,128)(2,1)S(1)}, u32[]{:S(2)}, u32[]{:S(2)}) collective-permute-start(bf16[256,64]{0,1:T(8,128)(2,1)S(1)} %get-tuple-element.14), channel_id=1, source_target_pairs={{0,1},{1,0},{2,3},{3,2},{4,5},{5,4},{6,7},{7,6},{8,9},{9,8},{10,11... | collective-permute-start | bytes 98312 | tf_op jit(solution)/shard_map/ppermute | solution.py:16
  12.3 1.9 collective-permute-done.1
  16.6 2.0 fusion.3
  20.6 8.6 %collective-permute-done.2 = bf16[512,256]{0,1:T(8,128)(2,1)S(1)} collective-permute-done((bf16[512,256]{0,1:T(8,128)(2,1)S(1)}, bf16[512,256]{0,1:T(8,128)(2,1)S(1)}, u32[]{:S(2)}, u32[]{:S(2)}) %collective-permute-start.2) | collective-permute-done | bytes 262176 | tf_op jit(solution)/shard_map/ppermute | solution.py:72
  29.9 8.8 %collective-permute-done.3 = bf16[512,256]{0,1:T(8,128)(2,1)S(1)} collective-permute-done((bf16[512,256]{0,1:T(8,128)(2,1)S(1)}, bf16[512,256]{0,1:T(8,128)(2,1)S(1)}, u32[]{:S(2)}, u32[]{:S(2)}) %collective-permute-start.3) | collective-permute-done | bytes 262176 | tf_op jit(solution)/shard_map/ppermute | solution.py:72
  39.5 10.0 %collective-permute-done.4 = bf16[512,256]{0,1:T(8,128)(2,1)S(1)} collective-permute-done((bf16[512,256]{0,1:T(8,128)(2,1)S(1)}, bf16[512,256]{0,1:T(8,128)(2,1)S(1)}, u32[]{:S(2)}, u32[]{:S(2)}) %collective-permute-start.4) | collective-permute-done | bytes 262176 | tf_op jit(solution)/shard_map/ppermute | solution.py:72
  50.2 8.5 %collective-permute-done.5 = bf16[512,256]{0,1:T(8,128)(2,1)S(1)} collective-permute-done((bf16[512,256]{0,1:T(8,128)(2,1)S(1)}, bf16[512,256]{0,1:T(8,128)(2,1)S(1)}, u32[]{:S(2)}, u32[]{:S(2)}) %collective-permute-start.5) | collective-permute-done | bytes 262176 | tf_op jit(solution)/shard_map/ppermute | solution.py:72
  59.4 8.5 %collective-permute-done.6 = bf16[512,256]{0,1:T(8,128)(2,1)S(1)} collective-permute-done((bf16[512,256]{0,1:T(8,128)(2,1)S(1)}, bf16[512,256]{0,1:T(8,128)(2,1)S(1)}, u32[]{:S(2)}, u32[]{:S(2)}) %collective-permute-start.6) | collective-permute-done | bytes 262176 | tf_op jit(solution)/shard_map/ppermute | solution.py:72
  68.6 8.5 %collective-permute-done.7 = bf16[512,256]{0,1:T(8,128)(2,1)S(1)} collective-permute-done((bf16[512,256]{0,1:T(8,128)(2,1)S(1)}, bf16[512,256]{0,1:T(8,128)(2,1)S(1)}, u32[]{:S(2)}, u32[]{:S(2)}) %collective-permute-start.7) | collective-permute-done | bytes 262176 | tf_op jit(solution)/shard_map/ppermute | solution.py:72
  77.8 8.5 %collective-permute-done.8 = bf16[512,256]{0,1:T(8,128)(2,1)S(1)} collective-permute-done((bf16[512,256]{0,1:T(8,128)(2,1)S(1)}, bf16[512,256]{0,1:T(8,128)(2,1)S(1)}, u32[]{:S(2)}, u32[]{:S(2)}) %collective-permute-start.8) | collective-permute-done | bytes 262176 | tf_op jit(solution)/shard_map/ppermute | solution.py:72
  87.0 8.5 %collective-permute-done.9 = bf16[512,256]{0,1:T(8,128)(2,1)S(1)} collective-permute-done((bf16[512,256]{0,1:T(8,128)(2,1)S(1)}, bf16[512,256]{0,1:T(8,128)(2,1)S(1)}, u32[]{:S(2)}, u32[]{:S(2)}) %collective-permute-start.9) | collective-permute-done | bytes 262176 | tf_op jit(solution)/shard_map/ppermute | solution.py:72
  96.2 8.5 %collective-permute-done.10 = bf16[512,256]{0,1:T(8,128)(2,1)S(1)} collective-permute-done((bf16[512,256]{0,1:T(8,128)(2,1)S(1)}, bf16[512,256]{0,1:T(8,128)(2,1)S(1)}, u32[]{:S(2)}, u32[]{:S(2)}) %collective-permute-start.10) | collective-permute-done | bytes 262176 | tf_op jit(solution)/shard_map/ppermute | solution.py:72
  105.4 8.5 %collective-permute-done.11 = bf16[512,256]{0,1:T(8,128)(2,1)S(1)} collective-permute-done((bf16[512,256]{0,1:T(8,128)(2,1)S(1)}, bf16[512,256]{0,1:T(8,128)(2,1)S(1)}, u32[]{:S(2)}, u32[]{:S(2)}) %collective-permute-start.11) | collective-permute-done | bytes 262176 | tf_op jit(solution)/shard_map/ppermute | solution.py:72
  114.6 14.0 %collective-permute-done.12 = bf16[512,256]{0,1:T(8,128)(2,1)S(1)} collective-permute-done((bf16[512,256]{0,1:T(8,128)(2,1)S(1)}, bf16[512,256]{0,1:T(8,128)(2,1)S(1)}, u32[]{:S(2)}, u32[]{:S(2)}) %collective-permute-start.12) | collective-permute-done | bytes 262176 | tf_op jit(solution)/shard_map/ppermute | solution.py:72
  129.3 8.7 %collective-permute-done.13 = bf16[512,256]{0,1:T(8,128)(2,1)S(1)} collective-permute-done((bf16[512,256]{0,1:T(8,128)(2,1)S(1)}, bf16[512,256]{0,1:T(8,128)(2,1)S(1)}, u32[]{:S(2)}, u32[]{:S(2)}) %collective-permute-start.13) | collective-permute-done | bytes 262176 | tf_op jit(solution)/shard_map/ppermute | solution.py:72
  138.7 2.4 collective-permute-start
  141.1 10.5 %collective-permute-done.14 = bf16[512,256]{0,1:T(8,128)(2,1)S(1)} collective-permute-done((bf16[512,256]{0,1:T(8,128)(2,1)S(1)}, bf16[512,256]{0,1:T(8,128)(2,1)S(1)}, u32[]{:S(2)}, u32[]{:S(2)}) %collective-permute-start.14) | collective-permute-done | bytes 262176 | tf_op jit(solution)/shard_map/ppermute | solution.py:72
  154.5 7.8 %collective-permute-done.15 = bf16[512,256]{0,1:T(8,128)(2,1)} collective-permute-done((bf16[512,256]{0,1:T(8,128)(2,1)S(1)}, bf16[512,256]{0,1:T(8,128)(2,1)}, u32[]{:S(2)}, u32[]{:S(2)}) %collective-permute-start.15) | collective-permute-done | bytes 262176 | tf_op jit(solution)/shard_map/ppermute | solution.py:72
  162.4 3.4 %convolution_bitcast_fusion = f32[384,1,128]{0,2,1:T(8,128)S(1)} fusion(bf16[4096,128]{0,1:T(8,128)(2,1)} %all-gather.9.cloned.1.call-done, bf16[384,4096]{1,0:T(8,128)(2,1)} %all-gather.7.cloned.1.call-done), kind=kOutput, calls=%fused_computation.13 | convolution fusion | flops 402653184 | bytes 4390912 | tf_op jit(solution)/shard_map/dot_general | solution.py:88
  166.3 4.8 %collective-permute-done.16 = bf16[512,256]{0,1:T(8,128)(2,1)} collective-permute-done((bf16[512,256]{0,1:T(8,128)(2,1)}, bf16[512,256]{0,1:T(8,128)(2,1)}, u32[]{:S(2)}, u32[]{:S(2)}) %collective-permute-start.16) | collective-permute-done | bytes 262176 | tf_op jit(solution)/shard_map/ppermute | solution.py:72
  171.1 1.7 constant_dynamic-update-slice_fusion.31
  172.8 1.7 constant_dynamic-update-slice_fusion.30
  174.5 1.7 constant_dynamic-update-slice_fusion.29
  177.8 1.7 constant_dynamic-update-slice_fusion.27
  179.5 1.7 constant_dynamic-update-slice_fusion.26
  181.1 1.7 constant_dynamic-update-slice_fusion.25
  190.9 1.7 constant_dynamic-update-slice_fusion.14
  195.5 1.7 constant_dynamic-update-slice_fusion.9
  203.8 4.6 %fusion.39 = f32[512,384]{1,0:T(8,128)S(1)} fusion(bf16[4096,512]{1,0:T(8,128)(2,1)} %all-gather.11.cloned.1.call-done, bf16[384,4096]{1,0:T(8,128)(2,1)S(1)} %copy-done.1), kind=kOutput, calls=%fused_computation.113 | convolution fusion | flops 1610612736 | bytes 8126464 | tf_op jit(solution)/shard_map/dot_general | solution.py:87
  211.6 4.1 %convolution_convert_fusion.1 = bf16[128,4,384]{2,0,1:T(8,128)(2,1)S(1)} fusion(f32[384,384,4]{1,0,2:T(8,128)S(1)} %get-tuple-element.16, f32[4,384]{1,0:T(4,128)S(1)} %fusion.1, f32[4,384]{1,0:T(4,128)S(1)} %get-tuple-element.15, pred[384,384]{0,1:T(8,128)(4,1)S(1)} %copy-done.2, bf16[4096,128]{0,1:T(8,128)(2,1)} %all-gather.5.cloned.1.call-done, ...), kind=kOutput, calls=%fused_computation.7 | convolution fusion | flops 556843008 | bytes 7106560 | tf_op jit(solution)/shard_map/chqk,ckd->cqhd/dot_general | solution.py:109
  215.7 5.7 %convolution_convert_fusion = bf16[384,4096]{1,0:T(8,128)(2,1)} fusion(bf16[384,512]{0,1:T(8,128)(2,1)S(1)} %bitcast.59, bf16[512,8192]{0,1:T(8,128)(2,1)} %constant_dynamic-update-slice_fusion, s32[]{:T(128)S(6)} %select_n.88), kind=kOutput, calls=%fused_computation | convolution fusion | flops 1612185600 | bytes 7733252 | tf_op jit(solution)/shard_map/dot_general | solution.py:113
  221.4 40.7 %reduce-scatter.2.cloned.1.call-done = bf16[192,4096]{1,0:T(8,128)(2,1)} async-done(((bf16[384,4096]{1,0:T(8,128)(2,1)}), bf16[192,4096]{1,0:T(8,128)(2,1)}) %reduce-scatter.2.cloned.1.call-update) | async-done | bytes 1572880 | tf_op jit(solution)/shard_map/reduce_scatter | solution.py:114
  (133 shorter events, 41.3 us)
Async XLA Ops:
  6.5 155.8 %all-gather.9.cloned.1.call-start = ((), (), s32[]{:S(2)}) async-start(), calls=%async_computation.3 | async-start | bytes 1114112 | tf_op jit(solution)/shard_map/all_gather | solution.py:84
  9.3 4.9 %collective-permute-start.1 = (bf16[256,64]{0,1:T(8,128)(2,1)S(1)}, bf16[256,64]{0,1:T(8,128)(2,1)S(1)}, u32[]{:S(2)}, u32[]{:S(2)}) collective-permute-start(bf16[256,64]{0,1:T(8,128)(2,1)S(1)} %get-tuple-element.14), channel_id=1, source_target_pairs={{0,1},{1,0},{2,3},{3,2},{4,5},{5,4},{6,7},{7,6},{8,9},{9,8},{10,11... | collective-permute-start | bytes 98312 | tf_op jit(solution)/shard_map/ppermute | solution.py:16
  14.8 147.5 %all-gather.7.cloned.1.call-start = ((), (), s32[]{:S(2)}) async-start(), calls=%async_computation.2 | async-start | bytes 4718592 | tf_op jit(solution)/shard_map/all_gather | solution.py:76
  15.6 188.2 %all-gather.11.cloned.1.call-start = ((), (), s32[]{:S(2)}) async-start(), calls=%async_computation.4 | async-start | bytes 4456448 | tf_op jit(solution)/shard_map/all_gather | solution.py:83
  18.6 192.9 %all-gather.5.cloned.1.call-start = ((), (), s32[]{:S(2)}) async-start(), calls=%async_computation.1 | async-start | bytes 1114112 | tf_op jit(solution)/shard_map/all_gather | solution.py:85
  20.6 8.7 %collective-permute-start.2 = (bf16[512,256]{0,1:T(8,128)(2,1)S(1)}, bf16[512,256]{0,1:T(8,128)(2,1)S(1)}, u32[]{:S(2)}, u32[]{:S(2)}) collective-permute-start(bf16[512,256]{0,1:T(8,128)(2,1)S(1)} %fusion.4), channel_id=1, source_target_pairs={{0,2},{2,4},{4,6},{6,8},{8,10},{10,12},{12,14},{14,16},{16,18},{18... | collective-permute-start | bytes 786440 | tf_op jit(solution)/shard_map/ppermute | solution.py:72
  29.9 8.8 %collective-permute-start.3 = (bf16[512,256]{0,1:T(8,128)(2,1)S(1)}, bf16[512,256]{0,1:T(8,128)(2,1)S(1)}, u32[]{:S(2)}, u32[]{:S(2)}) collective-permute-start(bf16[512,256]{0,1:T(8,128)(2,1)S(1)} %collective-permute-done.2), channel_id=1, source_target_pairs={{0,2},{2,4},{4,6},{6,8},{8,10},{10,12},{12,14},{14,16},{16,18},{18... | collective-permute-start | bytes 786440 | tf_op jit(solution)/shard_map/ppermute | solution.py:72
  39.5 10.0 %collective-permute-start.4 = (bf16[512,256]{0,1:T(8,128)(2,1)S(1)}, bf16[512,256]{0,1:T(8,128)(2,1)S(1)}, u32[]{:S(2)}, u32[]{:S(2)}) collective-permute-start(bf16[512,256]{0,1:T(8,128)(2,1)S(1)} %collective-permute-done.3), channel_id=1, source_target_pairs={{0,2},{2,4},{4,6},{6,8},{8,10},{10,12},{12,14},{14,16},{16,18},{18... | collective-permute-start | bytes 786440 | tf_op jit(solution)/shard_map/ppermute | solution.py:72
  50.2 8.5 %collective-permute-start.5 = (bf16[512,256]{0,1:T(8,128)(2,1)S(1)}, bf16[512,256]{0,1:T(8,128)(2,1)S(1)}, u32[]{:S(2)}, u32[]{:S(2)}) collective-permute-start(bf16[512,256]{0,1:T(8,128)(2,1)S(1)} %collective-permute-done.4), channel_id=1, source_target_pairs={{0,2},{2,4},{4,6},{6,8},{8,10},{10,12},{12,14},{14,16},{16,18},{18... | collective-permute-start | bytes 786440 | tf_op jit(solution)/shard_map/ppermute | solution.py:72
  59.4 8.5 %collective-permute-start.6 = (bf16[512,256]{0,1:T(8,128)(2,1)S(1)}, bf16[512,256]{0,1:T(8,128)(2,1)S(1)}, u32[]{:S(2)}, u32[]{:S(2)}) collective-permute-start(bf16[512,256]{0,1:T(8,128)(2,1)S(1)} %collective-permute-done.5), channel_id=1, source_target_pairs={{0,2},{2,4},{4,6},{6,8},{8,10},{10,12},{12,14},{14,16},{16,18},{18... | collective-permute-start | bytes 786440 | tf_op jit(solution)/shard_map/ppermute | solution.py:72
  68.6 8.5 %collective-permute-start.7 = (bf16[512,256]{0,1:T(8,128)(2,1)S(1)}, bf16[512,256]{0,1:T(8,128)(2,1)S(1)}, u32[]{:S(2)}, u32[]{:S(2)}) collective-permute-start(bf16[512,256]{0,1:T(8,128)(2,1)S(1)} %collective-permute-done.6), channel_id=1, source_target_pairs={{0,2},{2,4},{4,6},{6,8},{8,10},{10,12},{12,14},{14,16},{16,18},{18... | collective-permute-start | bytes 786440 | tf_op jit(solution)/shard_map/ppermute | solution.py:72
  77.8 8.5 %collective-permute-start.8 = (bf16[512,256]{0,1:T(8,128)(2,1)S(1)}, bf16[512,256]{0,1:T(8,128)(2,1)S(1)}, u32[]{:S(2)}, u32[]{:S(2)}) collective-permute-start(bf16[512,256]{0,1:T(8,128)(2,1)S(1)} %collective-permute-done.7), channel_id=1, source_target_pairs={{0,2},{2,4},{4,6},{6,8},{8,10},{10,12},{12,14},{14,16},{16,18},{18... | collective-permute-start | bytes 786440 | tf_op jit(solution)/shard_map/ppermute | solution.py:72
  87.0 8.5 %collective-permute-start.9 = (bf16[512,256]{0,1:T(8,128)(2,1)S(1)}, bf16[512,256]{0,1:T(8,128)(2,1)S(1)}, u32[]{:S(2)}, u32[]{:S(2)}) collective-permute-start(bf16[512,256]{0,1:T(8,128)(2,1)S(1)} %collective-permute-done.8), channel_id=1, source_target_pairs={{0,2},{2,4},{4,6},{6,8},{8,10},{10,12},{12,14},{14,16},{16,18},{18... | collective-permute-start | bytes 786440 | tf_op jit(solution)/shard_map/ppermute | solution.py:72
  96.2 8.5 %collective-permute-start.10 = (bf16[512,256]{0,1:T(8,128)(2,1)S(1)}, bf16[512,256]{0,1:T(8,128)(2,1)S(1)}, u32[]{:S(2)}, u32[]{:S(2)}) collective-permute-start(bf16[512,256]{0,1:T(8,128)(2,1)S(1)} %collective-permute-done.9), channel_id=1, source_target_pairs={{0,2},{2,4},{4,6},{6,8},{8,10},{10,12},{12,14},{14,16},{16,18},{18... | collective-permute-start | bytes 786440 | tf_op jit(solution)/shard_map/ppermute | solution.py:72
  105.4 8.5 %collective-permute-start.11 = (bf16[512,256]{0,1:T(8,128)(2,1)S(1)}, bf16[512,256]{0,1:T(8,128)(2,1)S(1)}, u32[]{:S(2)}, u32[]{:S(2)}) collective-permute-start(bf16[512,256]{0,1:T(8,128)(2,1)S(1)} %collective-permute-done.10), channel_id=1, source_target_pairs={{0,2},{2,4},{4,6},{6,8},{8,10},{10,12},{12,14},{14,16},{16,18},{18... | collective-permute-start | bytes 786440 | tf_op jit(solution)/shard_map/ppermute | solution.py:72
  114.6 14.0 %collective-permute-start.12 = (bf16[512,256]{0,1:T(8,128)(2,1)S(1)}, bf16[512,256]{0,1:T(8,128)(2,1)S(1)}, u32[]{:S(2)}, u32[]{:S(2)}) collective-permute-start(bf16[512,256]{0,1:T(8,128)(2,1)S(1)} %collective-permute-done.11), channel_id=1, source_target_pairs={{0,2},{2,4},{4,6},{6,8},{8,10},{10,12},{12,14},{14,16},{16,18},{18... | collective-permute-start | bytes 786440 | tf_op jit(solution)/shard_map/ppermute | solution.py:72
  129.3 8.7 %collective-permute-start.13 = (bf16[512,256]{0,1:T(8,128)(2,1)S(1)}, bf16[512,256]{0,1:T(8,128)(2,1)S(1)}, u32[]{:S(2)}, u32[]{:S(2)}) collective-permute-start(bf16[512,256]{0,1:T(8,128)(2,1)S(1)} %collective-permute-done.12), channel_id=1, source_target_pairs={{0,2},{2,4},{4,6},{6,8},{8,10},{10,12},{12,14},{14,16},{16,18},{18... | collective-permute-start | bytes 786440 | tf_op jit(solution)/shard_map/ppermute | solution.py:72
  138.7 12.9 %collective-permute-start.14 = (bf16[512,256]{0,1:T(8,128)(2,1)S(1)}, bf16[512,256]{0,1:T(8,128)(2,1)S(1)}, u32[]{:S(2)}, u32[]{:S(2)}) collective-permute-start(bf16[512,256]{0,1:T(8,128)(2,1)S(1)} %collective-permute-done.13), channel_id=1, source_target_pairs={{0,2},{2,4},{4,6},{6,8},{8,10},{10,12},{12,14},{14,16},{16,18},{18... | collective-permute-start | bytes 786440 | tf_op jit(solution)/shard_map/ppermute | solution.py:72
  138.7 15.1 %collective-permute-start = (bf16[256,64]{0,1:T(8,128)(2,1)S(1)}, bf16[256,64]{0,1:T(8,128)(2,1)S(1)}, u32[]{:S(2)}, u32[]{:S(2)}) collective-permute-start(bf16[256,64]{0,1:T(8,128)(2,1)S(1)} %get-tuple-element.13), channel_id=1, source_target_pairs={{0,1},{1,0},{2,3},{3,2},{4,5},{5,4},{6,7},{7,6},{8,9},{9,8},{10,11... | collective-permute-start | bytes 98312 | tf_op jit(solution)/shard_map/ppermute | solution.py:16
  151.6 10.7 %collective-permute-start.15 = (bf16[512,256]{0,1:T(8,128)(2,1)S(1)}, bf16[512,256]{0,1:T(8,128)(2,1)}, u32[]{:S(2)}, u32[]{:S(2)}) collective-permute-start(bf16[512,256]{0,1:T(8,128)(2,1)S(1)} %collective-permute-done.14), channel_id=1, source_target_pairs={{0,2},{2,4},{4,6},{6,8},{8,10},{10,12},{12,14},{14,16},{16,18},{18... | collective-permute-start | bytes 786440 | tf_op jit(solution)/shard_map/ppermute | solution.py:72
  154.5 107.7 %reduce-scatter.2.cloned.1.call-start = ((), (), s32[]{:S(2)}) async-start(), calls=%async_computation.5 | async-start | bytes 4718592 | tf_op jit(solution)/shard_map/reduce_scatter | solution.py:114
  162.3 8.8 %collective-permute-start.16 = (bf16[512,256]{0,1:T(8,128)(2,1)}, bf16[512,256]{0,1:T(8,128)(2,1)}, u32[]{:S(2)}, u32[]{:S(2)}) collective-permute-start(bf16[512,256]{0,1:T(8,128)(2,1)} %collective-permute-done.15), channel_id=1, source_target_pairs={{0,2},{2,4},{4,6},{6,8},{8,10},{10,12},{12,14},{14,16},{16,18},{18... | collective-permute-start | bytes 786440 | tf_op jit(solution)/shard_map/ppermute | solution.py:72
  162.4 22.6 %copy-start.12 = (bf16[512,256]{0,1:T(8,128)(2,1)S(1)}, bf16[512,256]{0,1:T(8,128)(2,1)}, u32[]{:S(2)}) copy-start(bf16[512,256]{0,1:T(8,128)(2,1)} %copy-done.11) | copy-start | bytes 786436
  162.4 23.3 %copy-start.10 = (bf16[512,256]{0,1:T(8,128)(2,1)S(1)}, bf16[512,256]{0,1:T(8,128)(2,1)}, u32[]{:S(2)}) copy-start(bf16[512,256]{0,1:T(8,128)(2,1)} %copy-done.9) | copy-start | bytes 786436
  162.4 24.0 %copy-start.8 = (bf16[512,256]{0,1:T(8,128)(2,1)S(1)}, bf16[512,256]{0,1:T(8,128)(2,1)}, u32[]{:S(2)}) copy-start(bf16[512,256]{0,1:T(8,128)(2,1)} %copy-done.7) | copy-start | bytes 786436
  162.4 24.7 %copy-start.6 = (bf16[512,256]{0,1:T(8,128)(2,1)S(1)}, bf16[512,256]{0,1:T(8,128)(2,1)}, u32[]{:S(2)}) copy-start(bf16[512,256]{0,1:T(8,128)(2,1)} %copy-done.5) | copy-start | bytes 786436
  162.4 25.4 %copy-start.4 = (bf16[512,256]{0,1:T(8,128)(2,1)S(1)}, bf16[512,256]{0,1:T(8,128)(2,1)}, u32[]{:S(2)}) copy-start(bf16[512,256]{0,1:T(8,128)(2,1)} %copy-done.3) | copy-start | bytes 786436
  162.4 31.0 %copy-start.25 = (bf16[512,256]{0,1:T(8,128)(2,1)S(1)}, bf16[512,256]{0,1:T(8,128)(2,1)}, u32[]{:S(2)}) copy-start(bf16[512,256]{0,1:T(8,128)(2,1)} %copy-done.24) | copy-start | bytes 786436
  162.4 31.7 %copy-start.23 = (bf16[512,256]{0,1:T(8,128)(2,1)S(1)}, bf16[512,256]{0,1:T(8,128)(2,1)}, u32[]{:S(2)}) copy-start(bf16[512,256]{0,1:T(8,128)(2,1)} %copy-done.22) | copy-start | bytes 786436
  162.4 32.4 %copy-start.21 = (bf16[512,256]{0,1:T(8,128)(2,1)S(1)}, bf16[512,256]{0,1:T(8,128)(2,1)}, u32[]{:S(2)}) copy-start(bf16[512,256]{0,1:T(8,128)(2,1)} %copy-done.20) | copy-start | bytes 786436
  166.3 26.3 %copy-start.27 = (bf16[512,256]{0,1:T(8,128)(2,1)S(1)}, bf16[512,256]{0,1:T(8,128)(2,1)}, u32[]{:S(2)}) copy-start(bf16[512,256]{0,1:T(8,128)(2,1)} %copy-done.26) | copy-start | bytes 786436
  166.3 37.5 %copy-start.1 = (bf16[384,4096]{1,0:T(8,128)(2,1)S(1)}, bf16[384,4096]{1,0:T(8,128)(2,1)}, u32[]{:S(2)}) copy-start(bf16[384,4096]{1,0:T(8,128)(2,1)} %all-gather.7.cloned.1.call-done) | copy-start | bytes 9437188
  (18 other events, 106.0 us)
Sparse Core Ops, SparseCore 0:
  14.9 39.7 all-gather.8
  56.2 46.5 all-gather.6
  105.0 54.7 all-gather.10
  161.8 36.8 all-gather.4
  221.5 40.5 reduce-scatter.1
